TPU v7x, 32 devices: a whole 2x2x4 slice. The times are simulated.
32 devices in a mesh: dp: 8 (over z, x), tensor: 4 (over y, core).
Axes of the slice: x: 2, y: 2, z: 4, core: 2. Of those that a mesh axis runs over, the one named last changes fastest.
Arguments:
- tokens: bfloat16 [24576, 512], P(('dp', 'tensor')), may hold values from -6 to 6
- lengths: int32 [16, 4], P('dp'), may hold values from 1 to 768, 1536 in all within a row
- w_qkv: bfloat16 [512, 3, 512], P(None, None, 'tensor'), may hold values from -0.25 to 0.25
- w_out: bfloat16 [512, 512], P('tensor'), may hold values from -1 to 1
- w_up: bfloat16 [512, 2048], P(None, 'tensor'), may hold values from -0.25 to 0.25
- w_down: bfloat16 [2048, 512], P('tensor'), may hold values from -0.125 to 0.125
- w_pool: bfloat16 [1536, 512], replicated, may hold values from -0.15625 to 0.15625
- gain_one: float32 [512], replicated, may hold values from 0.5 to 1.5
- gain_two: float32 [512], replicated, may hold values from 0.5 to 1.5
- pooled_grad: bfloat16 [8192, 512], P(('dp', 'tensor')), may hold values from -6 to 6
Outputs:
- pooled: bfloat16 [8192, 512], P(('dp', 'tensor'))
- rms_block: float32 [], replicated
- rms_pool: float32 [], replicated
- grad_tokens: bfloat16 [24576, 512], P(('dp', 'tensor'))
- grad_qkv: float32 [512, 3, 512], P(None, None, 'tensor')
- grad_out: float32 [512, 512], P('tensor')
- grad_up: float32 [512, 2048], P(None, 'tensor')
- grad_down: float32 [2048, 512], P('tensor')
- grad_pool: float32 [1536, 512], replicated
- grad_gain_one: float32 [512], replicated
- grad_gain_two: float32 [512], replicated
Inputs may be any that keep to these rules, and one draw needn't show every extreme that they name: Each row holds 4 sequences whose lengths sum to 1536; the longest of every row is exactly 768.
All inputs are finite; a program needn't handle non-finite values.
Results may differ from a plain program's by a relative error of at most 0.018.
Values may be sent and summed in bfloat16 or wider, within the bound.
A program may use at most 256 MiB of HBM per device.

v0:
```python
import math

import jax
import jax.numpy as jnp
from jax import lax
from jax.sharding import PartitionSpec as P

HEAD = 64
POOL = 3


EPS = 1e-06
NEG = -1000000000.0


def passed_along(block, axis, distance):
    devices = range(lax.axis_size(axis))
    route = [(i - distance, i) for i in devices if i - distance in devices]
    return lax.ppermute(block, axis, route)


def rms_scale(hidden):
    return lax.rsqrt(jnp.mean(hidden * hidden, axis=1, keepdims=True) + EPS)


def norm_apply(hidden, gain):
    return hidden * rms_scale(hidden) * gain


def doc_table(lengths, row_len):
    seg_ends = jnp.cumsum(lengths, axis=1)
    position = jnp.arange(row_len, dtype=jnp.int32)
    in_row = jnp.sum((position[None, :, None] >= seg_ends[:, None, :]).astype(jnp.int32), axis=2)
    row_ids = jnp.arange(lengths.shape[0], dtype=jnp.int32)[:, None] * lengths.shape[1]
    return in_row + row_ids


def rotation(positions, head_size):
    half_size = head_size // 2
    frequency = jnp.exp(-math.log(10000.0) * jnp.arange(half_size, dtype=jnp.float32) / half_size)
    phase_angle = positions.astype(jnp.float32)[:, None, None] * frequency
    return (jnp.cos(phase_angle), jnp.sin(phase_angle))


def rotate(vectors, cosine, sine_part):
    half_size = vectors.shape[-1] // 2
    front_half = vectors[..., :half_size]
    back_half = vectors[..., half_size:]
    return jnp.concatenate(
        [front_half * cosine - back_half * sine_part, front_half * sine_part + back_half * cosine],
        axis=-1,
    )


def rotate_back(grads, cosine, sine_part):
    half_size = grads.shape[-1] // 2
    front_half = grads[..., :half_size]
    back_half = grads[..., half_size:]
    return jnp.concatenate(
        [front_half * cosine + back_half * sine_part, back_half * cosine - front_half * sine_part],
        axis=-1,
    )


def block_scores(queries, key_rows, query_pos, key_pos, query_docs, key_docs, scale):
    scores = (
        jnp.einsum("qhe,khe->hqk", queries, key_rows, preferred_element_type=jnp.float32) * scale
    )
    allowed = (key_pos[None, :] <= query_pos[:, None]) & (key_docs[None, :] == query_docs[:, None])
    return (queries, jnp.where(allowed[None], scores, NEG))


def attend(queries, key_rows, values, query_pos, key_pos, query_docs, key_docs, block_len, scale):

    def one_block(row_start):
        query_block, scores = block_scores(
            queries, key_rows, query_pos, key_pos, query_docs, key_docs, scale
        )
        row_max = jnp.max(scores, axis=2, keepdims=True)
        exp_scores = jnp.exp(scores - row_max)
        row_total = jnp.sum(exp_scores, axis=2, keepdims=True)
        attn_probs = (exp_scores / row_total).astype(jnp.bfloat16)
        mixed = jnp.einsum("hqk,khe->qhe", attn_probs, values, preferred_element_type=jnp.float32)
        return (mixed, (row_max + jnp.log(row_total))[:, :, 0])

    starts = jnp.arange(queries.shape[0] // block_len, dtype=jnp.int32) * block_len
    mixed, log_total = lax.map(one_block, starts)
    return (mixed.reshape(queries.shape), log_total)


def attend_back(
    queries,
    key_rows,
    values,
    query_pos,
    key_pos,
    query_docs,
    key_docs,
    log_total,
    grad_mixed,
    block_len,
    scale,
):

    def one_block(carry, inputs):
        grad_keys, grad_values = carry
        row_start, block_total = inputs
        query_block, scores = block_scores(
            queries, key_rows, query_pos, key_pos, query_docs, key_docs, scale
        )
        attn_probs = jnp.exp(scores - block_total[:, :, None])
        grad_probs = jnp.einsum(
            "qhe,khe->hqk", grad_mixed, values, preferred_element_type=jnp.float32
        )
        inner = jnp.sum(attn_probs * grad_probs, axis=2, keepdims=True)
        grad_scores = (attn_probs * (grad_probs - inner)).astype(jnp.bfloat16)
        grad_query = (
            jnp.einsum("hqk,khe->qhe", grad_scores, key_rows, preferred_element_type=jnp.float32)
            * scale
        )
        grad_keys = (
            grad_keys
            + jnp.einsum(
                "hqk,qhe->khe", grad_scores, query_block, preferred_element_type=jnp.float32
            )
            * scale
        )
        grad_values = grad_values + jnp.einsum(
            "hqk,qhe->khe",
            attn_probs.astype(jnp.bfloat16),
            grad_mixed,
            preferred_element_type=jnp.float32,
        )
        return ((grad_keys, grad_values), grad_query)

    zeros = jnp.zeros(key_rows.shape, jnp.float32)
    starts = jnp.arange(queries.shape[0] // block_len, dtype=jnp.int32) * block_len
    (grad_keys, grad_values), grad_queries = lax.scan(
        one_block, (zeros, zeros), (starts, log_total)
    )
    return (grad_queries.reshape(queries.shape), grad_keys, grad_values)


def gelu_tanh(pre_act):
    return jax.nn.gelu(pre_act, approximate=True)


def shards(tokens, lengths, w_qkv, w_out, w_up, w_down, w_pool, gain_one, gain_two, pooled_grad):
    shard_rows, width = tokens.shape
    tensor_size = lax.axis_size("tensor")
    tensor_rank = lax.axis_index("tensor")
    micro_count = lengths.shape[0]
    group_rows = shard_rows * tensor_size
    row_len = group_rows // micro_count
    scale = HEAD ** (-0.5)
    rim_len = POOL - 1
    local_cols = w_qkv.shape[2]
    local_units = w_up.shape[1]
    row_docs = doc_table(lengths, row_len)
    flat_docs = row_docs.reshape(group_rows)
    local_start = tensor_rank * shard_rows
    local_docs = lax.dynamic_slice_in_dim(flat_docs, local_start, shard_rows, 0)
    padded_docs = jnp.concatenate([jnp.full((rim_len,), -1, jnp.int32), flat_docs])
    prev_docs = lax.dynamic_slice_in_dim(padded_docs, local_start, shard_rows, 0)
    keep_rows = (prev_docs == local_docs)[:, None]
    tokens_f = tokens.astype(jnp.float32)
    normed_one = norm_apply(tokens_f, gain_one).astype(jnp.bfloat16)
    qkv_full, out_full, up_full, down_full = (
        lax.all_gather(w_qkv, "tensor", axis=2, tiled=True),
        lax.all_gather(w_out, "tensor", axis=0, tiled=True),
        lax.all_gather(w_up, "tensor", axis=1, tiled=True),
        lax.all_gather(w_down, "tensor", axis=0, tiled=True),
    )
    full_cols = qkv_full.shape[2]
    head_count = full_cols // HEAD
    block_len = math.gcd(shard_rows, 768)
    group_pos = local_start + jnp.arange(shard_rows, dtype=jnp.int32)
    cosine, sine_part = rotation(group_pos % row_len, HEAD)
    local_heads = (shard_rows, head_count, HEAD)
    projected = jnp.einsum("td,dcf->tcf", normed_one, qkv_full, preferred_element_type=jnp.float32)
    queries = rotate(projected[:, 0].reshape(local_heads), cosine, sine_part).astype(jnp.bfloat16)
    key_rows = rotate(projected[:, 1].reshape(local_heads), cosine, sine_part).astype(jnp.bfloat16)
    values = projected[:, 2].reshape(local_heads).astype(jnp.bfloat16)
    before_keys, before_values = passed_along((key_rows, values), "tensor", 1)
    keys_all = jnp.concatenate([before_keys, key_rows], axis=0)
    values_all = jnp.concatenate([before_values, values], axis=0)
    long_docs = jnp.concatenate([jnp.full((shard_rows,), -1, jnp.int32), flat_docs])
    before_docs = lax.dynamic_slice_in_dim(long_docs, local_start, shard_rows, 0)
    key_docs = jnp.concatenate([before_docs, local_docs])
    key_pos = jnp.concatenate([group_pos - shard_rows, group_pos])
    mixed, log_total = attend(
        queries, keys_all, values_all, group_pos, key_pos, local_docs, key_docs, block_len, scale
    )
    mixed_heads = mixed.reshape(shard_rows, full_cols).astype(jnp.bfloat16)
    hidden_one = tokens_f + jnp.dot(mixed_heads, out_full, preferred_element_type=jnp.float32)
    normed_two = norm_apply(hidden_one, gain_two).astype(jnp.bfloat16)
    pre_act = jnp.dot(normed_two, up_full, preferred_element_type=jnp.float32)
    activated = gelu_tanh(pre_act).astype(jnp.bfloat16)
    hidden_two = hidden_one + jnp.dot(activated, down_full, preferred_element_type=jnp.float32)
    hidden_low = hidden_two.astype(jnp.bfloat16)
    rim_rows = passed_along(hidden_low[shard_rows - rim_len :], "tensor", 1)
    candidate = jnp.concatenate([rim_rows, hidden_low[: shard_rows - rim_len]], axis=0)
    shifted = jnp.where(keep_rows, candidate, jnp.zeros_like(candidate))
    pool_in = shifted.reshape(shard_rows // POOL, POOL * width)
    pooled = jnp.dot(pool_in, w_pool, preferred_element_type=jnp.float32)
    block_square = jnp.sum(hidden_two * hidden_two)
    pool_square = jnp.sum(pooled * pooled)
    grad_pool = jnp.einsum("rk,rd->kd", pool_in, pooled_grad, preferred_element_type=jnp.float32)
    grad_shift = jnp.einsum(
        "rd,kd->rk", pooled_grad, w_pool, preferred_element_type=jnp.float32
    ).reshape(shard_rows, width)
    grad_shift = jnp.where(keep_rows, grad_shift, jnp.zeros_like(grad_shift))
    rim_grad = passed_along(grad_shift[:rim_len], "tensor", -1)
    grad_two = jnp.concatenate([grad_shift[rim_len:], rim_grad], axis=0)
    grad_branch = grad_two.astype(jnp.bfloat16)
    gelu_out, gelu_back = jax.vjp(gelu_tanh, pre_act)
    grad_down_full = jnp.einsum(
        "tf,td->fd", activated, grad_branch, preferred_element_type=jnp.float32
    )
    grad_act = jnp.einsum("td,fd->tf", grad_branch, down_full, preferred_element_type=jnp.float32)
    grad_pre = gelu_back(grad_act)[0].astype(jnp.bfloat16)
    grad_up_full = jnp.einsum("td,tf->df", normed_two, grad_pre, preferred_element_type=jnp.float32)
    grad_normed = jnp.einsum("tf,df->td", grad_pre, up_full, preferred_element_type=jnp.float32)
    norm_out, norm_back = jax.vjp(norm_apply, hidden_one, gain_two)
    grad_hidden, grad_gain_two = norm_back(grad_normed)
    grad_one = grad_two + grad_hidden
    grad_attn = grad_one.astype(jnp.bfloat16)
    dp_size = lax.axis_size("dp")
    grad_out_full = jnp.einsum(
        "tf,td->fd", mixed_heads, grad_attn, preferred_element_type=jnp.float32
    )
    grad_mixed = (
        jnp.einsum("td,fd->tf", grad_attn, out_full, preferred_element_type=jnp.float32)
        .astype(jnp.bfloat16)
        .reshape(local_heads)
    )
    grad_queries, grad_keys_all, grad_values_all = attend_back(
        queries,
        keys_all,
        values_all,
        group_pos,
        key_pos,
        local_docs,
        key_docs,
        log_total,
        grad_mixed,
        block_len,
        scale,
    )
    back_keys, back_values = (
        passed_along(grad_keys_all[:shard_rows].astype(jnp.bfloat16), "tensor", -1).astype(
            jnp.float32
        ),
        passed_along(grad_values_all[:shard_rows].astype(jnp.bfloat16), "tensor", -1).astype(
            jnp.float32
        ),
    )
    grad_keys = grad_keys_all[shard_rows:] + back_keys
    grad_values = grad_values_all[shard_rows:] + back_values
    grad_queries = rotate_back(grad_queries, cosine, sine_part).reshape(shard_rows, full_cols)
    grad_keys = rotate_back(grad_keys, cosine, sine_part).reshape(shard_rows, full_cols)
    grad_values = grad_values.reshape(shard_rows, full_cols)
    grad_proj = jnp.stack([grad_queries, grad_keys, grad_values], axis=1).astype(jnp.bfloat16)
    grad_qkv_full = jnp.einsum(
        "td,tcf->dcf", normed_one, grad_proj, preferred_element_type=jnp.float32
    )
    grad_normed_one = jnp.einsum(
        "tcf,dcf->td", grad_proj, qkv_full, preferred_element_type=jnp.float32
    )
    first_out, first_back = jax.vjp(norm_apply, tokens_f, gain_one)
    grad_input, grad_gain_one = first_back(grad_normed_one)
    grad_tokens = (grad_one + grad_input).astype(jnp.bfloat16)
    summed = lax.psum(
        (
            grad_qkv_full,
            grad_out_full,
            grad_up_full,
            grad_down_full,
            grad_pool,
            grad_gain_one,
            grad_gain_two,
            block_square,
            pool_square,
        ),
        ("dp", "tensor"),
    )
    grad_qkv = lax.dynamic_slice_in_dim(summed[0], tensor_rank * local_cols, local_cols, 2)
    grad_out = lax.dynamic_slice_in_dim(summed[1], tensor_rank * local_cols, local_cols, 0)
    grad_up = lax.dynamic_slice_in_dim(summed[2], tensor_rank * local_units, local_units, 1)
    grad_down = lax.dynamic_slice_in_dim(summed[3], tensor_rank * local_units, local_units, 0)
    grad_pool, grad_gain_one, grad_gain_two, block_square, pool_square = (
        summed[4],
        summed[5],
        summed[6],
        summed[7],
        summed[8],
    )
    rms_block = jnp.sqrt(block_square / (group_rows * dp_size * width))
    rms_pool = jnp.sqrt(pool_square / (group_rows // POOL * dp_size * width))
    return (
        pooled.astype(jnp.bfloat16),
        rms_block,
        rms_pool,
        grad_tokens,
        grad_qkv,
        grad_out,
        grad_up,
        grad_down,
        grad_pool,
        grad_gain_one,
        grad_gain_two,
    )


def solution(mesh):
    placed = (
        P(("dp", "tensor"), None),
        P("dp", None),
        P(None, None, "tensor"),
        P("tensor", None),
        P(None, "tensor"),
        P("tensor", None),
        P(),
        P(),
        P(),
        P(("dp", "tensor"), None),
    )
    return jax.shard_map(
        shards,
        mesh=mesh,
        in_specs=placed,
        out_specs=(
            P(("dp", "tensor"), None),
            P(),
            P(),
            P(("dp", "tensor"), None),
            P(None, None, "tensor"),
            P("tensor", None),
            P(None, "tensor"),
            P("tensor", None),
            P(),
            P(),
            P(),
        ),
        check_vma=False,
    )
```

profile of v0, /device:TPU:0, one launch (start us, length us, event | category | flops | bytes accessed | tf_op | source)
XLA Modules:
  0.0 590.0 jit_solution(15449846273376132443)
XLA Ops:
  23.0 9.6 %all-gather.4.cloned.1.call-done = bf16[512,3,512]{0,2,1:T(8,128)(2,1)} async-done(((bf16[512,3,128]{0,2,1:T(8,128)(2,1)}), bf16[512,3,512]{0,2,1:T(8,128)(2,1)}) %all-gather.4.cloned.1.call-update) | async-done | bytes 1572880 | tf_op jit(solution)/shard_map/all_gather | solution.py:169
  32.7 2.9 fusion.34
  39.4 9.8 %all_gather.13 = bf16[512,512]{1,0:T(8,128)(2,1)} all-gather(bf16[128,512]{1,0:T(8,128)(2,1)S(1)} %copy-done.35), channel_id=1, replica_groups=mesh['dp'=8,'tensor'=4] {'tensor'}, dimensions={0}, use_global_device_ids=true | all-gather | bytes 655360 | tf_op jit(solution)/shard_map/all_gather | solution.py:170
  51.3 16.2 %collective-permute-start = (bf16[768,8,64]{0,2,1:T(8,128)(2,1)S(1)}, bf16[768,8,64]{0,2,1:T(8,128)(2,1)}, u32[]{:S(2)}, u32[]{:S(2)}) collective-permute-start(bf16[768,8,64]{0,2,1:T(8,128)(2,1)S(1)} %bitcast.57), channel_id=1, source_target_pairs={{0,1},{1,2},{2,3},{4,5},{5,6},{6,7},{8,9},{9,10},{10,11},{12,13},{... | collective-permute-start | bytes 2359304 | tf_op jit(solution)/shard_map/ppermute | solution.py:19
  68.4 18.3 %fusion.59 = (f32[8,768]{1,0:T(8,128)}, f32[8,768,1536]{2,1,0:T(8,128)}) fusion(bf16[768,8,32]{0,2,1:T(8,128)(2,1)S(1)} %get-tuple-element.111, bf16[768,8,32]{0,2,1:T(8,128)(2,1)S(1)} %get-tuple-element.112, bf16[768,8,64]{0,2,1:T(8,128)(2,1)} %copy-done.33, bf16[768,8,32]{0,2,1:T(8,128)(2,1)} %get-tuple-element.102, ...), kind=kOutput, calls=%fused_computation.126 | convolution fusion | flops 1242556416 | bytes 41312256 | tf_op jit(solution)/shard_map/while/body/eval_jaxpr/qhe,khe->hqk/dot_general | solution.py:67
  86.7 17.2 %fusion = f32[8,768]{1,0:T(8,128)S(1)} fusion(f32[8,768,1536]{2,1,0:T(8,128)} %get-tuple-element.116, f32[8,768]{1,0:T(8,128)} %get-tuple-element.115), kind=kLoop, calls=%fused_computation.6 | loop fusion | flops 18868224 | bytes 37797888 | tf_op jit(solution)/shard_map/while/body/eval_jaxpr/reduce_sum | solution.py:81
  104.0 15.0 %fusion.27 = bf16[8,64,768]{2,1,0:T(8,128)(2,1)S(1)} fusion(f32[8,768,1536]{2,1,0:T(8,128)} %get-tuple-element.116, f32[8,768]{1,0:T(8,128)S(1)} %fusion, f32[8,768]{1,0:T(8,128)S(1)} %copy-done.37, bf16[768,8,64]{0,2,1:T(8,128)(2,1)S(1)} %bitcast.58, bf16[768,8,64]{0,2,1:T(8,128)(2,1)} %collective-permute-done), kind=kOutput, calls=%fused_computation.61 | convolution fusion | flops 1239810048 | bytes 40157184 | tf_op jit(solution)/shard_map/while/body/eval_jaxpr/hqk,khe->qhe/dot_general | solution.py:83
  119.9 6.7 %fusion.57 = f32[768,2048]{1,0:T(8,128)} fusion(bf16[512,2048]{1,0:T(8,128)(2,1)} %all-gather.6.cloned.1.call-done, f32[768,512]{1,0:T(8,128)S(1)} %get-tuple-element.118, f32[512]{0:T(512)S(1)} %copy-done.36, f32[768]{0:T(1024)S(1)} %fusion.46), kind=kOutput, calls=%fused_computation.124 | convolution fusion | flops 1611792384 | bytes 9966592 | tf_op jit(solution)/shard_map/dot_general | solution.py:197
  126.6 6.6 %multiply_reduce_fusion.3 = (f32[]{:T(128)}, bf16[768,512]{1,0:T(8,128)(2,1)S(1)}) fusion(f32[768,512]{1,0:T(8,128)S(1)} %get-tuple-element.118, bf16[2048,512]{1,0:T(8,128)(2,1)} %all-gather.8.cloned.1.call-done, f32[768,2048]{1,0:T(8,128)} %fusion.57), kind=kOutput, calls=%fused_computation.55 | convolution fusion | flops 1626341376 | bytes 10747908 | tf_op jit(solution)/shard_map/dot_general | solution.py:199
  133.2 4.9 collective-permute-start.2
  138.2 5.5 fusion.12
  143.7 4.0 fusion.56
  153.2 16.8 %fusion.14 = f32[1536,8,64]{0,2,1:T(8,128)} fusion(bf16[768,8,64]{0,2,1:T(8,128)(2,1)} %bitcast.53, f32[8,768,1536]{2,1,0:T(8,128)} %get-tuple-element.116, f32[8,768]{1,0:T(8,128)S(1)} %log_add_fusion), kind=kOutput, calls=%fused_computation.24 | convolution fusion | flops 1226833920 | bytes 41705472 | tf_op jit(solution)/shard_map/while/body/eval_jaxpr/hqk,qhe->khe/dot_general | solution.py:128
  173.7 28.8 %multiply_reduce_fusion = (f32[8,768]{1,0:T(8,128)S(1)}, f32[8,768,1536]{2,1,0:T(8,128)}) fusion(f32[8,768,1536]{2,1,0:T(8,128)} %get-tuple-element.116, f32[8,768]{1,0:T(8,128)S(1)} %log_add_fusion, bf16[768,8,64]{0,2,1:T(8,128)(2,1)} %bitcast.54, bf16[768,8,64]{0,2,1:T(8,128)(2,1)} %bitcast.59, bf16[768,8,64]{0,2,1:T(8,128)(2,1)} %collective-permute-done), kind=kOutput, calls=%fused_computation.1 | convolution fusion | flops 1239410688 | bytes 77905920 | tf_op jit(solution)/shard_map/while/body/eval_jaxpr/qhe,khe->hqk/dot_general | solution.py:112
  202.5 31.3 %multiply_convert_fusion = bf16[8,768,1536]{2,1,0:T(8,128)(2,1)} fusion(f32[8,768,1536]{2,1,0:T(8,128)} %get-tuple-element.123, f32[8,768,1536]{2,1,0:T(8,128)} %get-tuple-element.116, f32[8,768]{1,0:T(8,128)S(1)} %get-tuple-element.122, f32[8,768]{1,0:T(8,128)S(1)} %log_add_fusion), kind=kLoop, calls=%fused_computation | loop fusion | flops 37748736 | bytes 94420992 | tf_op jit(solution)/shard_map/while/body/eval_jaxpr/convert_element_type | solution.py:116
  233.8 8.5 %fusion.13 = f32[1536,8,64]{0,2,1:T(8,128)S(1)} fusion(bf16[8,768,1536]{2,1,0:T(8,128)(2,1)} %multiply_convert_fusion, bf16[768,8,32]{0,2,1:T(8,128)(2,1)} %get-tuple-element.102, bf16[768,8,32]{0,2,1:T(8,128)(2,1)} %copy-done.23), kind=kOutput, calls=%fused_computation.23 | convolution fusion | flops 1210318848 | bytes 22806528 | tf_op jit(solution)/shard_map/while/body/eval_jaxpr/hqk,qhe->khe/dot_general | solution.py:123
  246.6 7.6 %fusion.39 = f32[2048,512]{1,0:T(8,128)} fusion(f32[2,512]{1,0:T(2,128)S(1)} %collective-permute-done.3, f32[766,512]{1,0:T(8,128)S(1)} %copy-done.12, f32[768,2048]{1,0:T(8,128)} %fusion.57), kind=kOutput, calls=%fused_computation.88 | convolution fusion | flops 1626341376 | bytes 12058624 | tf_op jit(solution)/shard_map/tf,td->fd/dot_general | solution.py:217
  254.2 11.0 %multiply_bitcast_fusion = f32[768,8,64]{0,2,1:T(8,128)} fusion(bf16[8,768,1536]{2,1,0:T(8,128)(2,1)} %multiply_convert_fusion, bf16[768,8,32]{0,2,1:T(8,128)(2,1)S(1)} %copy-done.14, bf16[768,8,32]{0,2,1:T(8,128)(2,1)S(1)} %copy-done.16, bf16[768,8,64]{0,2,1:T(8,128)(2,1)S(1)} %copy-done.34), kind=kOutput, calls=%fused_computation.53 | convolution fusion | flops 1213071360 | bytes 22020096 | tf_op jit(solution)/shard_map/while/body/eval_jaxpr/hqk,khe->qhe/dot_general | solution.py:118
  292.3 5.0 fusion.30
  297.4 3.2 multiply_reduce_fusion.5
  300.6 4.3 fusion.20
  304.9 44.9 %all-reduce.2 = (f32[]{:T(128)}, f32[]{:T(128)}, f32[512]{0:T(512)}, f32[512]{0:T(512)}) all-reduce(f32[]{:T(128)} %get-tuple-element.105, f32[]{:T(128)} %get-tuple-element.107, f32[512]{0:T(512)S(1)} %get-tuple-element.69, f32[512]{0:T(512)S(1)} %get-tuple-element.67), channel_id=1, replica_groups=mesh['dp'=8,'tensor'=4] {'dp','tensor'}, use_global_device_ids=true, to_apply=%region_7.8 | all-reduce | flops 1026 | bytes 8208 | tf_op jit(solution)/shard_map/psum | solution.py:273
  351.2 3.1 fusion.23
  354.3 216.6 %all-reduce.6.cloned.1.call-done = (f32[512,3,512]{2,0,1:T(8,128)}, f32[512,512]{1,0:T(8,128)}, f32[512,2048]{1,0:T(8,128)}, f32[2048,512]{1,0:T(8,128)}, f32[1536,512]{1,0:T(8,128)}) async-done(((f32[512,3,512]{2,0,1:T(8,128)}, f32[512,512]{1,0:T(8,128)}, f32[512,2048]{1,0:T(8,128)}, f32[2048,512]{1,0:T(8,128)}, f32[1536,512]{1,0:T(8,128)}), (f32[512,3,512]{2,0,1:T(8,128)}, f32[512,512]{1,0:T(8,128)}, ...) | async-done | bytes 15728656 | tf_op jit(solution)/shard_map/psum | solution.py:273
  (170 shorter events, 73.9 us)
Async XLA Ops:
  7.2 25.5 %all-gather.4.cloned.1.call-start = ((), (), s32[]{:S(2)}) async-start(), calls=%async_computation | async-start | bytes 1966080 | tf_op jit(solution)/shard_map/all_gather | solution.py:169
  9.3 110.6 %all-gather.6.cloned.1.call-start = ((), (), s32[]{:S(2)}) async-start(), calls=%async_computation.1 | async-start | bytes 2621440 | tf_op jit(solution)/shard_map/all_gather | solution.py:171
  10.0 116.5 %all-gather.8.cloned.1.call-start = ((), (), s32[]{:S(2)}) async-start(), calls=%async_computation.2 | async-start | bytes 2621440 | tf_op jit(solution)/shard_map/all_gather | solution.py:172
  16.9 121.2 %collective-permute-start.3 = (f32[2,512]{1,0:T(2,128)S(1)}, f32[2,512]{1,0:T(2,128)S(1)}, u32[]{:S(2)}, u32[]{:S(2)}) collective-permute-start(f32[2,512]{1,0:T(2,128)S(1)} %slice.89), channel_id=1, source_target_pairs={{1,0},{2,1},{3,2},{5,4},{6,5},{7,6},{9,8},{10,9},{11,10},{13,12},{... | collective-permute-start | bytes 12296 | tf_op jit(solution)/shard_map/ppermute | solution.py:19
  18.4 552.6 %all-reduce.6.cloned.1.call-start = ((), (), s32[]{:S(2)}) async-start(), calls=%async_computation.3 | async-start | bytes 31457280 | tf_op jit(solution)/shard_map/psum | solution.py:273
  18.7 14.0 %copy-start.42 = (f32[512]{0:T(512)S(1)}, f32[512]{0:T(512)}, u32[]{:S(2)}) copy-start(f32[512]{0:T(512)} %param.17) | copy-start | bytes 6148
  21.8 13.8 %copy-start.40 = (f32[768]{0:T(1024)}, f32[768]{0:T(1024)S(1)}, u32[]{:S(2)}) copy-start(f32[768]{0:T(1024)S(1)} %fusion.44) | copy-start | bytes 9220
  23.0 12.8 %copy-start.25 = (f32[768,32]{0,1:T(8,128)}, f32[768,32]{0,1:T(8,128)S(1)}, u32[]{:S(2)}) copy-start(f32[768,32]{0,1:T(8,128)S(1)} %get-tuple-element.113) | copy-start | bytes 294916
  23.0 12.8 %copy-start.27 = (f32[768,32]{0,1:T(8,128)}, f32[768,32]{0,1:T(8,128)S(1)}, u32[]{:S(2)}) copy-start(f32[768,32]{0,1:T(8,128)S(1)} %get-tuple-element.114) | copy-start | bytes 294916
  37.1 31.3 %copy-start.13 = (bf16[768,8,32]{0,2,1:T(8,128)(2,1)}, bf16[768,8,32]{0,2,1:T(8,128)(2,1)S(1)}, u32[]{:S(2)}) copy-start(bf16[768,8,32]{0,2,1:T(8,128)(2,1)S(1)} %get-tuple-element.111) | copy-start | bytes 1179652
  37.1 31.3 %copy-start.15 = (bf16[768,8,32]{0,2,1:T(8,128)(2,1)}, bf16[768,8,32]{0,2,1:T(8,128)(2,1)S(1)}, u32[]{:S(2)}) copy-start(bf16[768,8,32]{0,2,1:T(8,128)(2,1)S(1)} %get-tuple-element.112) | copy-start | bytes 1179652
  37.1 31.3 %copy-start.23 = (bf16[768,8,32]{0,2,1:T(8,128)(2,1)}, bf16[768,8,32]{0,2,1:T(8,128)(2,1)S(1)}, u32[]{:S(2)}) copy-start(bf16[768,8,32]{0,2,1:T(8,128)(2,1)S(1)} %get-tuple-element.101) | copy-start | bytes 1179652
  37.1 30.4 %collective-permute-start.1 = (bf16[768,8,64]{0,2,1:T(8,128)(2,1)S(1)}, bf16[768,8,64]{0,2,1:T(8,128)(2,1)S(1)}, u32[]{:S(2)}, u32[]{:S(2)}) collective-permute-start(bf16[768,8,64]{0,2,1:T(8,128)(2,1)S(1)} %pad_maximum_fusion.8), channel_id=1, source_target_pairs={{0,1},{1,2},{2,3},{4,5},{5,6},{6,7},{8,9},{9,10},{10,11},{12,13},{... | collective-permute-start | bytes 2359304 | tf_op jit(solution)/shard_map/ppermute | solution.py:19
  51.3 52.6 %copy-start.17 = (bf16[768,1,512]{0,2,1:T(8,128)(2,1)}, bf16[768,1,512]{0,2,1:T(8,128)(2,1)S(1)}, u32[]{:S(2)}) copy-start(bf16[768,1,512]{0,2,1:T(8,128)(2,1)S(1)} %slice.123) | copy-start | bytes 2359300
  51.3 52.6 %collective-permute-start = (bf16[768,8,64]{0,2,1:T(8,128)(2,1)S(1)}, bf16[768,8,64]{0,2,1:T(8,128)(2,1)}, u32[]{:S(2)}, u32[]{:S(2)}) collective-permute-start(bf16[768,8,64]{0,2,1:T(8,128)(2,1)S(1)} %bitcast.57), channel_id=1, source_target_pairs={{0,1},{1,2},{2,3},{4,5},{5,6},{6,7},{8,9},{9,10},{10,11},{12,13},{... | collective-permute-start | bytes 2359304 | tf_op jit(solution)/shard_map/ppermute | solution.py:19
  86.7 17.3 %copy-start.37 = (f32[8,768]{1,0:T(8,128)S(1)}, f32[8,768]{1,0:T(8,128)}, u32[]{:S(2)}) copy-start(f32[8,768]{1,0:T(8,128)} %get-tuple-element.115) | copy-start | bytes 73732
  103.9 15.1 %copy-start.7 = (bf16[768,512]{1,0:T(8,128)(2,1)S(1)}, bf16[768,512]{1,0:T(8,128)(2,1)}, u32[]{:S(2)}) copy-start(bf16[768,512]{1,0:T(8,128)(2,1)} %param.10) | copy-start | bytes 2359300
  103.9 15.1 %copy-start.20 = (bf16[512,512]{1,0:T(8,128)(2,1)S(1)}, bf16[512,512]{1,0:T(8,128)(2,1)}, u32[]{:S(2)}) copy-start(bf16[512,512]{1,0:T(8,128)(2,1)} %all_gather.13) | copy-start | bytes 1572868
  119.9 27.8 %copy-start.2 = (f32[768,512]{1,0:T(8,128)}, f32[768,512]{1,0:T(8,128)S(1)}, u32[]{:S(2)}) copy-start(f32[768,512]{1,0:T(8,128)S(1)} %get-tuple-element.118) | copy-start | bytes 4718596
  133.2 133.6 %collective-permute-start.2 = (bf16[2,512]{1,0:T(2,128)(2,1)S(1)}, bf16[2,512]{1,0:T(2,128)(2,1)S(1)}, u32[]{:S(2)}, u32[]{:S(2)}) collective-permute-start(bf16[2,512]{1,0:T(2,128)(2,1)S(1)} %slice.86), channel_id=1, source_target_pairs={{0,1},{1,2},{2,3},{4,5},{5,6},{6,7},{8,9},{9,10},{10,11},{12,13},{... | collective-permute-start | bytes 6152 | tf_op jit(solution)/shard_map/ppermute | solution.py:19
  172.4 103.4 %collective-permute-start.5 = (bf16[768,8,64]{0,2,1:T(8,128)(2,1)}, bf16[768,8,64]{0,2,1:T(8,128)(2,1)}, u32[]{:S(2)}, u32[]{:S(2)}) collective-permute-start(bf16[768,8,64]{0,2,1:T(8,128)(2,1)} %slice.121), channel_id=1, source_target_pairs={{1,0},{2,1},{3,2},{5,4},{6,5},{7,6},{9,8},{10,9},{11,10},{13,12},{... | collective-permute-start | bytes 2359304 | tf_op jit(solution)/shard_map/ppermute | solution.py:19
  233.8 12.8 %copy-start.12 = (f32[766,512]{1,0:T(8,128)S(1)}, f32[766,512]{1,0:T(8,128)}, u32[]{:S(2)}) copy-start(f32[766,512]{1,0:T(8,128)} %slice.88) | copy-start | bytes 4706308
  245.0 36.4 %collective-permute-start.4 = (bf16[768,8,64]{0,2,1:T(8,128)(2,1)}, bf16[768,8,64]{0,2,1:T(8,128)(2,1)}, u32[]{:S(2)}, u32[]{:S(2)}) collective-permute-start(bf16[768,8,64]{0,2,1:T(8,128)(2,1)} %slice.122), channel_id=1, source_target_pairs={{1,0},{2,1},{3,2},{5,4},{6,5},{7,6},{9,8},{10,9},{11,10},{13,12},{... | collective-permute-start | bytes 2359304 | tf_op jit(solution)/shard_map/ppermute | solution.py:19
  300.6 50.6 %copy-start.39 = (f32[768]{0:T(1024)S(1)}, f32[768]{0:T(1024)}, u32[]{:S(2)}) copy-start(f32[768]{0:T(1024)} %copy-done.38) | copy-start | bytes 9220
  (32 other events, 151.7 us)
Sparse Core Ops, SparseCore 0:
  10.2 22.4 all-gather.3
  34.2 25.7 all-gather.5
  61.6 28.2 all-gather.7
  297.5 273.4 all-reduce.5
where the time goes:
time: 596 us; the launch traced here: 590 us
  waiting for transfers between devices  227 us (38%)
  matrix products  155 us (26%)
  other arithmetic  69.5 us (12%)
  blocking collectives  54.7 us (9%)
  local copies, waits for them, and re-layouts  38 us (6%)
  starting transfers between devices  27.8 us (5%)
  between operations  18.2 us (3%)
    psum x1, waiting for transfers between devices, shards(): lax.psum((grad_qkv_full, grad_out_full, grad_up_full, grad_down_full, gra...  217 us
    psum x1, blocking collectives, shards(): lax.psum((grad_qkv_full, grad_out_full, grad_up_full, grad_down_full, gra...  44.9 us
    convert_element_type x1, other arithmetic, one_block(): grad_scores = (attn_probs * (grad_probs - inner)).astype(jnp.bfloat16)  31.3 us
    dot_general x1, matrix products, one_block(): jnp.einsum('qhe,khe->hqk', grad_mixed, values, preferred_element_type=jnp...  28.8 us
    ppermute x6, starting transfers between devices, passed_along(): return lax.ppermute(block, axis, route)  27.6 us
    dot_general x1, matrix products, block_scores(): jnp.einsum('qhe,khe->hqk', queries, key_rows, preferred_element_type=jnp....  18.3 us
    reduce_sum x1, other arithmetic, one_block(): row_total = jnp.sum(exp_scores, axis=2, keepdims=True)  17.2 us
    dot_general x1, matrix products, one_block(): jnp.einsum('hqk,qhe->khe', attn_probs.astype(jnp.bfloat16), grad_mixed, p...  16.8 us
  transfers between devices with their start and end apart: 10, of which 2 were waited for; matrix products, arithmetic and copies ran while one was open for 39% of the time, Pallas kernels for 0%

commit v1 on v0

v1 whole, which is shorter than its diff:
```python
import functools
import math
from types import SimpleNamespace

import jax
import jax.numpy as jnp
import numpy as np
from jax import lax
from jax.experimental import pallas as pl
from jax.experimental.pallas import tpu as pltpu
from jax.sharding import PartitionSpec as P

HEAD = 64
POOL = 3
EPS = 1e-06
BIG = float(2**30)
NEG = -1000000000.0
BLOCK = 256
LEFT = 3
F32, BF16 = jnp.float32, jnp.bfloat16
MESH = pl.DeviceIdType.MESH


def dot(a, b, ca=1, cb=0):
    return lax.dot_general(a, b, (((ca,), (cb,)), ((), ())), preferred_element_type=F32)


def part(ref, dim, start, count):
    index = [slice(None)] * len(ref.shape)
    index[dim] = pl.ds(start, count)
    return ref.at[tuple(index)]


def wide(ref, start, count):
    return jnp.concatenate([ref[i, pl.ds(start, count), :] for i in range(ref.shape[0])], axis=1)


def put_wide(ref, start, count, value, stride=None):
    for i in range(ref.shape[0]):
        ref[i, pl.ds(start, count, stride=stride), :] = value[:, i * 128 : (i + 1) * 128]


class Links:
    def __init__(self, send, recv):
        self.send, self.recv, self.sent = send, recv, []

    def copy(self, src, dst, to):
        k = len(self.sent)
        move = pltpu.make_async_remote_copy(
            src, dst, self.send.at[k], self.recv.at[k], device_id=to, device_id_type=MESH
        )
        move.start()
        self.sent.append([move, False])
        return k

    def arrived(self, k):
        self.sent[k][0].wait_recv()

    def left(self, k):
        if not self.sent[k][1]:
            self.sent[k][0].wait_send()
            self.sent[k][1] = True

    def finish(self):
        for k in range(len(self.sent)):
            self.left(k)


class Loads:
    def __init__(self, sems):
        self.sems, self.moves = sems, []

    def copy(self, src, dst):
        move = pltpu.make_async_copy(src, dst, self.sems.at[len(self.moves)])
        move.start()
        self.moves.append([move, False])
        return len(self.moves) - 1

    def wait(self, *ks):
        for k in ks:
            if not self.moves[k][1]:
                self.moves[k][0].wait()
                self.moves[k][1] = True

    def finish(self):
        self.wait(*range(len(self.moves)))


def step(*gens):
    for gen in gens:
        next(gen, None)


def drain(*gens):
    live = list(gens)
    while live:
        live = [gen for gen in live if next(gen, "end") != "end"]


def gathered(links, shard, buf, dim, size, xbit, to_y, to_x, to_core):
    half = size // 2
    start = pl.multiple_of(xbit * half, 16)
    by_y = links.copy(part(shard, dim, start, half), part(buf.at[1], dim, start, half), to_y)
    if to_core is not None:
        own = links.copy(shard, buf.at[2], to_core)
    yield 1
    links.arrived(by_y)
    by_x = links.copy(part(buf.at[1], dim, start, half), part(buf.at[1], dim, start, half), to_x)
    yield 1
    links.arrived(by_x)
    if to_core is not None:
        other = links.copy(buf.at[1], buf.at[3], to_core)
        yield 1
        links.arrived(own)
        links.arrived(other)


def reduced(links, loads, acc, dim, size, halves, swaps, bufs, out):
    lo, n, spans = 0, size, []
    bufs = iter(bufs)
    for to, bit in halves:
        half = n // 2
        buf = next(bufs)
        there = pl.multiple_of(lo + (1 - bit) * half, 16)
        here = pl.multiple_of(lo + bit * half, 16)
        k = links.copy(part(acc, dim, there, half), buf, to)
        yield 1
        links.arrived(k)
        mine = part(acc, dim, here, half)
        mine[...] = mine[...] + buf[...]
        spans.append((to, lo))
        lo, n = here, half
    mine = part(acc, dim, lo, n)
    for to in swaps:
        buf = next(bufs)
        k = links.copy(mine, buf, to)
        yield 1
        links.arrived(k)
        links.left(k)
        mine[...] = mine[...] + buf[...]
    own = loads.copy(mine, part(out, dim, lo, n))
    src = mine
    for to, before in reversed(spans):
        k = links.copy(src, part(out, dim, lo, n), to)
        yield 1
        links.arrived(k)
        loads.wait(own)
        lo, n = before, 2 * n
        src = part(out, dim, lo, n)


def from_y(links, other, buf, own, to_y, rest):
    k = links.copy(other, buf, to_y)
    yield 1
    links.arrived(k)
    own[...] = own[...] + buf[...]
    yield from rest()


def summed(links, terms, bufs, partners):
    for i, to in enumerate(partners):
        k = links.copy(terms.at[i], bufs.at[i], to)
        yield 1
        links.arrived(k)
        terms[i + 1] = terms[i] + bufs[i]


def scratch_list(T, D, HC, U, bits):
    L, heads, qb = 2 * T, 2 * HC // HEAD, 2 * T // BLOCK
    blocks = sum(min(i, LEFT) + 1 for i in range(qb))
    kd = POOL * D
    halves, swaps = min(bits, 2), max(bits - 2, 0)

    def stages(rows, count):
        return [rows >> (i + 1) for i in range(count)]

    out = [
        ("xb", (T, D), BF16),
        ("nrm", (L, D), BF16),
        ("wq", (2, 3, D, HC), BF16),
        ("wqt", (6 * HC, D), BF16),
        ("wo", (4, HC, D), BF16),
        ("wu", (4, D, U), BF16),
        ("wd", (4, U, D), BF16),
        ("wp", (kd, D), BF16),
        ("pg", (T // POOL, D), BF16),
        ("cos", (HEAD // 2, L), F32),
        ("sin", (HEAD // 2, L), F32),
        ("qxt", (heads, 2 * HEAD, L), BF16),
        ("kt", (heads, HEAD, L), BF16),
        ("vt", (heads, HEAD, L), BF16),
        ("kx", (heads, L, 2 * HEAD), BF16),
        ("vx", (heads, L, 2 * HEAD), BF16),
        ("probs", (heads, blocks * BLOCK, BLOCK), BF16),
        ("rl", (heads, 8, L), F32),
        ("ot", (2 * HC, L), BF16),
        ("otf", (4 * HC, T), BF16),
        ("gox", (heads, 2 * HEAD, L), BF16),
        ("gpt", (6 * HC, L), BF16),
        ("h1", (T, D), F32),
        ("h2", (D // 128, T + 8, 128), F32),
        ("g2t", (D // 128, T + 8, 128), F32),
        ("rim", (D // 128, 8, 128), F32),
        ("n2", (T, D), BF16),
        ("act", (T, U), BF16),
        ("gpre", (T, U), BF16),
        ("gn", (T, D), F32),
        ("gatt", (L, D), BF16),
        ("pns", (T, D), BF16),
        ("pnr", (T, D), BF16),
        ("dk", (2, HEAD, L), F32),
        ("dv", (2, HEAD, L), F32),
        ("dq", (2, HEAD, L), F32),
        ("pool_in", (T // POOL, kd), BF16),
        ("pool_b", (T // POOL, D), BF16),
        ("gtok", (T, D), BF16),
        ("gd", (4, U, D), BF16),
        ("gu", (4, D, U), BF16),
        ("gq", (2, 3, D, HC), BF16),
        ("go", (2, HC, D), BF16),
        ("gp", (kd, D), BF16),
        ("cd", (2, U, D), BF16),
        ("cu", (2, D, U), BF16),
        ("yd", (U, D), BF16),
        ("yu", (D, U), BF16),
        ("yq", (3, D, HC), BF16),
        ("yo", (HC, D), BF16),
        ("terms", (bits + 3, 8, D), F32),
        ("term_in", (bits + 2, 8, D), F32),
    ]
    for name, rows, shape in (
        ("rd", U, lambda n: (n, D)),
        ("ru", D, lambda n: (n, U)),
        ("rq", D, lambda n: (3, n, HC)),
        ("ro", HC, lambda n: (n, D)),
    ):
        sizes = stages(rows, halves)
        sizes += [sizes[-1]] * swaps
        out += [(f"{name}{i}", shape(n), BF16) for i, n in enumerate(sizes)]
    sizes = stages(kd, 2 + halves)
    sizes += [sizes[-1]] * swaps
    out += [(f"rp{i}", (n, D), BF16) for i, n in enumerate(sizes)]
    return out


def kernel(bits, names, *refs):
    s = SimpleNamespace(**dict(zip(names, refs)))
    T, D = s.xb.shape
    HC, U = s.wo.shape[1], s.wu.shape[2]
    L, QB = 2 * T, 2 * T // BLOCK
    half_head = HEAD // 2
    RC = 64
    links, loads = Links(s.send_sems, s.recv_sems), Loads(s.load_sems)

    d, t = lax.axis_index("dp"), lax.axis_index("tensor")
    c, y = t % 2, t // 2
    to_core, to_y = (d, t + 1 - 2 * c), (d, t + 2 - 4 * y)
    bit = [(d // (1 << i)) % 2 for i in range(bits)]
    to_bit = [(d + (1 - 2 * bit[i]) * (1 << i), t) for i in range(bits)]
    halves = [(to_bit[i], bit[i]) for i in range(min(bits, 2))]
    swaps = to_bit[2:]
    mine = pl.multiple_of(c * T, T)
    theirs = pl.multiple_of((1 - c) * T, T)

    in_x = loads.copy(s.tokens, s.xb)
    in_q = loads.copy(s.w_qkv, s.wq.at[0])
    in_pool = loads.copy(s.w_pool, s.wp)
    in_pg = loads.copy(s.pooled_grad, s.pg)
    in_cos, in_sin = loads.copy(s.cos_in, s.cos), loads.copy(s.sin_in, s.sin)
    in_out = loads.copy(s.w_out, s.wo.at[0])
    in_up = loads.copy(s.w_up, s.wu.at[0])
    in_down = loads.copy(s.w_down, s.wd.at[0])

    partners = [to_core, to_y] + to_bit
    barrier = pltpu.get_barrier_semaphore()
    for to in partners:
        pl.semaphore_signal(barrier, inc=1, device_id=to, device_id_type=MESH)
    pl.semaphore_wait(barrier, len(partners))

    get_q = gathered(links, s.w_qkv, s.wq, 1, D, bit[0], to_y, to_bit[0], None)
    step(get_q)

    gain_one, gain_two = s.gain_one[...], s.gain_two[...]
    loads.wait(in_x)
    for r in range(0, T, RC):
        x = s.xb[r : r + RC, :].astype(F32)
        scale = lax.rsqrt(jnp.mean(x * x, axis=1, keepdims=True) + EPS)
        s.nrm[pl.ds(pl.multiple_of(mine + r, RC), RC), :] = (x * scale * gain_one).astype(BF16)
    own_rows = s.nrm.at[pl.ds(mine, T), :]
    sent_norm = links.copy(own_rows, own_rows, to_core)

    starts, ends, total = [], [], 0
    for j in range(4):
        starts.append(total)
        total = total + s.lengths[y, j]
        ends.append(total)

    def kept(j):
        p = mine + POOL * lax.broadcasted_iota(jnp.int32, (T // POOL, 1), 0) + j
        bad = (p - 1) <= 0
        for e in ends[:3]:
            bad = bad | ((p >= e) & (p - 1 <= e))
        return jnp.logical_not(bad)

    loads.wait(in_pool, in_pg)
    s.g2t[:, 0:8, :] = jnp.zeros((D // 128, 8, 128), F32)
    s.g2t[:, T : T + 8, :] = jnp.zeros((D // 128, 8, 128), F32)
    for j in range(POOL):
        grad_shift = dot(s.pg[...], s.wp[j * D : (j + 1) * D, :], 1, 1)
        put_wide(s.g2t, 8 - (POOL - 1) + j, T // POOL, jnp.where(kept(j), grad_shift, 0.0), POOL)
    sent_rim = links.copy(s.g2t.at[:, 0:8, :], s.rim, to_core)

    loads.wait(in_q, in_cos, in_sin)
    row = lax.broadcasted_iota(jnp.int32, (HEAD, L), 0)
    pos = lax.broadcasted_iota(jnp.int32, (HEAD, L), 1)
    same = jnp.zeros((HEAD, L), F32)
    for j in range(4):
        same = jnp.where((row == j) & (pos >= starts[j]) & (pos < ends[j]), 1.0, same)
    key_rows_doc = same.astype(BF16)
    query_rows_doc = jnp.where(row < 4, BIG * (same - 1.0), 0.0).astype(BF16)
    value_rows = jnp.where(row < 2, -1.0, 0.0).astype(BF16)
    for h in range(4):
        s.qxt[h, HEAD : 2 * HEAD, :] = query_rows_doc

    def turn_weights(slot):
        for i in range(3):
            s.wqt[(3 * slot + i) * HC : (3 * slot + i + 1) * HC, :] = s.wq[slot, i].T

    def project(slot, start):
        cols = pl.ds(start, T)
        cosine, sine = s.cos[:, cols], s.sin[:, cols]
        rows = s.nrm[cols, :]
        for i in range(3):
            r = dot(s.wqt[(3 * slot + i) * HC : (3 * slot + i + 1) * HC, :], rows, 1, 1)
            for h in range(2):
                u = r[h * HEAD : (h + 1) * HEAD, :]
                head = 2 * slot + h
                if i == 2:
                    s.vt[head, :, cols] = u.astype(BF16)
                    continue
                a, b = u[:half_head], u[half_head:]
                turned = jnp.concatenate([a * cosine - b * sine, a * sine + b * cosine], axis=0)
                if i == 0:
                    s.qxt[head, 0:HEAD, cols] = (turned * HEAD**-0.5).astype(BF16)
                else:
                    s.kt[head, :, cols] = turned.astype(BF16)

    def turn_keys(head):
        s.kx[head] = jnp.concatenate([s.kt[head], key_rows_doc], axis=0).T
        s.vx[head] = jnp.concatenate([s.vt[head], value_rows], axis=0).T

    turn_weights(0)
    project(0, mine)
    links.arrived(sent_norm)
    project(0, theirs)
    turn_keys(0)
    turn_keys(1)
    step(get_q)

    def fwd(head, qb):
        k0 = max(0, qb - LEFT)
        n = qb - k0 + 1
        off = sum(min(i, LEFT) + 1 for i in range(qb)) * BLOCK
        q = slice(qb * BLOCK, (qb + 1) * BLOCK)
        k = slice(k0 * BLOCK, (qb + 1) * BLOCK)
        scores = dot(s.kx[head, k, :], s.qxt[head, :, q])
        ki = lax.broadcasted_iota(jnp.int32, (BLOCK, BLOCK), 0)
        qi = lax.broadcasted_iota(jnp.int32, (BLOCK, BLOCK), 1)
        last = jnp.where(ki <= qi, scores[(n - 1) * BLOCK :], NEG)
        scores = last if n == 1 else jnp.concatenate([scores[: (n - 1) * BLOCK], last], axis=0)
        e = jnp.exp(scores - jnp.max(scores, axis=0, keepdims=True))
        inverse = 1.0 / jnp.sum(e, axis=0, keepdims=True)
        low = e.astype(BF16)
        s.probs[head, off : off + n * BLOCK, :] = low
        s.rl[head, 0:1, q] = inverse
        s.ot[pl.ds(pl.multiple_of(head * HEAD, HEAD), HEAD), q] = (dot(s.vt[head, :, k], low) * inverse).astype(BF16)

    def fwd_slot(slot):
        def one(h, _):
            for qb in range(QB):
                fwd(2 * slot + h, qb)
            return 0

        lax.fori_loop(0, 2, one, 0)

    def send_heads(slot):
        rows = slice(slot * HC, (slot + 1) * HC)
        s.otf[rows, :] = s.ot[rows, pl.ds(mine, T)]
        return links.copy(
            s.ot.at[rows, pl.ds(theirs, T)],
            s.otf.at[(2 + slot) * HC : (3 + slot) * HC, :],
            to_core,
        )

    fwd_slot(0)
    step(get_q)
    get_out = gathered(links, s.w_out, s.wo, 0, HC, bit[0], to_y, to_bit[0], to_core)
    get_up = gathered(links, s.w_up, s.wu, 0, D, bit[0], to_y, to_bit[0], to_core)
    get_down = gathered(links, s.w_down, s.wd, 0, U, bit[0], to_y, to_bit[0], to_core)
    step(get_out, get_up, get_down)
    turn_weights(1)
    project(1, mine)
    project(1, theirs)
    turn_keys(2)
    turn_keys(3)
    sent_heads = [send_heads(0)]
    step(get_out)
    step(get_out, get_up)
    fwd_slot(1)
    sent_heads.append(send_heads(1))
    step(get_up, get_down)
    drain(get_out)
    loads.wait(in_out)
    for k in sent_heads:
        links.arrived(k)

    wo = s.wo[...].reshape(4 * HC, D)
    s.h1[...] = dot(s.otf[...], wo, 0, 0)
    for r in range(0, T, RC):
        rows = slice(r, r + RC)
        h = s.h1[rows, :] + s.xb[rows, :].astype(F32)
        s.h1[rows, :] = h
        put_wide(s.h2, 8 + r, RC, h)
        scale = lax.rsqrt(jnp.mean(h * h, axis=1, keepdims=True) + EPS)
        s.n2[rows, :] = (h * scale * gain_two).astype(BF16)
    links.arrived(sent_rim)
    tail = lax.broadcasted_iota(jnp.int32, (D // 128, 8, 128), 1) >= 8 - (POOL - 1)
    s.g2t[:, T : T + 8, :] = s.g2t[:, T : T + 8, :] + jnp.where(tail, s.rim[...], 0.0)
    drain(get_up, get_down)
    loads.wait(in_up, in_down)

    root = math.sqrt(2.0 / math.pi)

    def feed_forward(slot, first):
        for r in range(0, T, BLOCK):
            rows = slice(r, r + BLOCK)
            v = dot(s.n2[rows, :], s.wu[slot])
            square = v * v
            th = jnp.tanh(root * v * (1.0 + 0.044715 * square))
            up = 0.5 * (1.0 + th)
            act = (v * up).astype(BF16)
            slope = up + 0.5 * v * (1.0 - th * th) * (root * (1.0 + 3 * 0.044715 * square))
            grad_act = dot(wide(s.g2t, 8 + r, BLOCK).astype(BF16), s.wd[slot], 1, 1)
            gpre = (grad_act * slope).astype(BF16)
            s.act[rows, :] = act
            s.gpre[rows, :] = gpre
            put_wide(s.h2, 8 + r, BLOCK, wide(s.h2, 8 + r, BLOCK) + dot(act, s.wd[slot]))
            grad_normed = dot(gpre, s.wu[slot], 1, 1)
            s.gn[rows, :] = grad_normed if first else s.gn[rows, :] + grad_normed
        s.gd[slot] = dot(s.act[...], wide(s.g2t, 8, T).astype(BF16), 0, 0).astype(BF16)
        s.gu[slot] = dot(s.n2[...], s.gpre[...], 0, 0).astype(BF16)

    def to_other_core(slot):
        return (
            links.copy(s.gd.at[slot], s.cd.at[slot - 2], to_core),
            links.copy(s.gu.at[slot], s.cu.at[slot - 2], to_core),
        )

    def from_other_core(slot, sent):
        links.arrived(sent[0])
        s.gd[slot] = s.gd[slot] + s.cd[slot]
        links.arrived(sent[1])
        s.gu[slot] = s.gu[slot] + s.cu[slot]

    def shard_sum(name, acc, dim, size, out):
        bufs = [getattr(s, f"{name}{i}") for i in range(bits)]
        return lambda: reduced(links, loads, acc, dim, size, halves, swaps, bufs, out)

    feed_forward(3, True)
    sent3 = to_other_core(3)
    feed_forward(1, False)
    from_other_core(1, sent3)
    sum_d = from_y(links, s.gd.at[1], s.yd, s.gd.at[0], to_y, shard_sum("rd", s.gd.at[0], 0, U, s.gd_out))
    sum_u = from_y(links, s.gu.at[1], s.yu, s.gu.at[0], to_y, shard_sum("ru", s.gu.at[0], 0, D, s.gu_out))
    step(sum_d, sum_u)
    feed_forward(2, False)
    sent2 = to_other_core(2)
    feed_forward(0, False)

    gain_grad_two = jnp.zeros((8, D), F32)
    for r in range(0, T, RC):
        rows = slice(r, r + RC)
        h, gn = s.h1[rows, :], s.gn[rows, :]
        scale = lax.rsqrt(jnp.mean(h * h, axis=1, keepdims=True) + EPS)
        e = gain_two * gn
        hs = h * scale
        grad = wide(s.g2t, 8 + r, RC) + scale * (e - hs * jnp.mean(e * hs, axis=1, keepdims=True))
        s.h1[rows, :] = grad
        s.gatt[pl.ds(pl.multiple_of(mine + r, RC), RC), :] = grad.astype(BF16)
        gain_grad_two = gain_grad_two + jnp.sum((gn * hs).reshape(RC // 8, 8, D), axis=0)
    own_rows = s.gatt.at[pl.ds(mine, T), :]
    sent_gatt = links.copy(own_rows, own_rows, to_core)
    sent_rim = links.copy(s.h2.at[:, T : T + 8, :], s.h2.at[:, 0:8, :], to_core)
    from_other_core(0, sent2)
    step(sum_d, sum_u)

    block_square = jnp.zeros((8, D), F32)
    for r in range(0, T, RC):
        h = wide(s.h2, 8 + r, RC)
        block_square = block_square + jnp.sum((h * h).reshape(RC // 8, 8, D), axis=0)
    links.arrived(sent_rim)
    for j in range(POOL):
        rows = pl.ds(8 - (POOL - 1) + j, T // POOL, stride=POOL)
        taken = jnp.concatenate([s.h2[i, rows, :] for i in range(D // 128)], axis=1)
        s.pool_in[:, j * D : (j + 1) * D] = jnp.where(kept(j), taken, 0.0).astype(BF16)
    pooled = dot(s.pool_in[...], s.wp[...])
    pool_square = jnp.sum((pooled * pooled).reshape(T // POOL // 8, 8, D), axis=0)
    s.pool_b[...] = pooled.astype(BF16)
    loads.copy(s.pool_b, s.pooled_out)
    for j in range(POOL):
        s.gp[j * D : (j + 1) * D, :] = dot(s.pool_in[:, j * D : (j + 1) * D], s.pg[...], 0, 0).astype(BF16)
    pool_halves = [(to_core, c), halves[0], (to_y, y)] + halves[1:]
    sum_p = reduced(
        links, loads, s.gp, 0, POOL * D, pool_halves, swaps,
        [getattr(s, f"rp{i}") for i in range(2 + bits)], s.gp_out,
    )
    step(sum_p)

    def grad_heads(start):
        cols = pl.ds(start, T)
        g = dot(s.wo[0:2].reshape(2 * HC, D), s.gatt[cols, :], 1, 1)
        line = lax.broadcasted_iota(jnp.int32, (HEAD, T), 0)
        for head in range(4):
            low = (g[head * HEAD : (head + 1) * HEAD] * s.rl[head, 0:1, cols]).astype(BF16)
            o = s.ot[head * HEAD : (head + 1) * HEAD, cols].astype(F32)
            delta = jnp.sum(low.astype(F32) * o, axis=0, keepdims=True)
            high = delta.astype(BF16).astype(F32)
            rest = jnp.where(line == 0, high, jnp.where(line == 1, delta - high, 0.0))
            s.gox[head, 0:HEAD, cols] = low
            s.gox[head, HEAD : 2 * HEAD, cols] = rest.astype(BF16)

    grad_heads(mine)
    links.arrived(sent_gatt)
    grad_heads(theirs)
    s.go[...] = dot(s.ot[...], s.gatt[...]).astype(BF16).reshape(2, HC, D)
    sum_o = from_y(links, s.go.at[1], s.yo, s.go.at[0], to_y, shard_sum("ro", s.go.at[0], 0, HC, s.go_out))
    step(sum_p, sum_o)

    def back(head, at, qb):
        k0 = max(0, qb - LEFT)
        n = qb - k0 + 1
        off = sum(min(i, LEFT) + 1 for i in range(qb)) * BLOCK
        q = slice(qb * BLOCK, (qb + 1) * BLOCK)
        k = slice(k0 * BLOCK, (qb + 1) * BLOCK)
        probs = s.probs[head, off : off + n * BLOCK, :]
        grad_scores = (probs.astype(F32) * dot(s.vx[head, k, :], s.gox[head, :, q])).astype(BF16)
        s.dq[at, :, q] = dot(s.kt[head, :, k], grad_scores)
        dk = dot(s.qxt[head, 0:HEAD, q], grad_scores, 1, 1)
        dv = dot(s.gox[head, 0:HEAD, q], probs, 1, 1)
        if n > 1:
            old = slice(k0 * BLOCK, qb * BLOCK)
            s.dk[at, :, old] = s.dk[at, :, old] + dk[:, : (n - 1) * BLOCK]
            s.dv[at, :, old] = s.dv[at, :, old] + dv[:, : (n - 1) * BLOCK]
        s.dk[at, :, q] = dk[:, (n - 1) * BLOCK :]
        s.dv[at, :, q] = dv[:, (n - 1) * BLOCK :]

    def back_head(slot, h):
        at = h
        for qb in range(QB):
            back(2 * slot + h, h, qb)
        cosine, sine = s.cos[...], s.sin[...]
        for i, (ref, factor) in enumerate(((s.dq, HEAD**-0.5), (s.dk, None))):
            a, b = ref[at, :half_head, :], ref[at, half_head:, :]
            turned = jnp.concatenate([a * cosine + b * sine, b * cosine - a * sine], axis=0)
            if factor is not None:
                turned = turned * factor
            s.gpt[pl.ds(pl.multiple_of((3 * slot + i) * HC + h * HEAD, HEAD), HEAD), :] = turned.astype(BF16)
        s.gpt[pl.ds(pl.multiple_of((3 * slot + 2) * HC + h * HEAD, HEAD), HEAD), :] = s.dv[at].astype(BF16)

    def back_slot(slot):
        def one(h, _):
            back_head(slot, h)
            return 0

        lax.fori_loop(0, 2, one, 0)

    def grad_weights(slot):
        for i in range(3):
            g = dot(s.gpt[(3 * slot + i) * HC : (3 * slot + i + 1) * HC, :], s.nrm[...])
            s.gq[slot, i] = g.astype(BF16).T

    back_slot(1)
    step(sum_d, sum_u, sum_p, sum_o)
    grad_weights(1)
    sum_q = from_y(links, s.gq.at[1], s.yq, s.gq.at[0], to_y, shard_sum("rq", s.gq.at[0], 1, D, s.gq_out))
    step(sum_q)
    back_slot(0)
    step(sum_d, sum_u, sum_p, sum_o)
    grad_weights(0)
    step(sum_q)

    s.pns[...] = dot(s.gpt[:, pl.ds(theirs, T)], s.wqt[...], 0, 0).astype(BF16)
    sent_pn = links.copy(s.pns, s.pnr, to_core)
    s.gn[...] = dot(s.gpt[:, pl.ds(mine, T)], s.wqt[...], 0, 0)
    step(sum_d, sum_u, sum_p, sum_o)
    links.arrived(sent_pn)
    gain_grad_one = jnp.zeros((8, D), F32)
    for r in range(0, T, RC):
        rows = slice(r, r + RC)
        x, gn = s.xb[rows, :].astype(F32), s.gn[rows, :] + s.pnr[rows, :].astype(F32)
        scale = lax.rsqrt(jnp.mean(x * x, axis=1, keepdims=True) + EPS)
        e = gain_one * gn
        xs = x * scale
        grad = s.h1[rows, :] + scale * (e - xs * jnp.mean(e * xs, axis=1, keepdims=True))
        s.gtok[rows, :] = grad.astype(BF16)
        gain_grad_one = gain_grad_one + jnp.sum((gn * xs).reshape(RC // 8, 8, D), axis=0)
    loads.copy(s.gtok, s.gtok_out)

    line = lax.broadcasted_iota(jnp.int32, (8, D), 0)
    small = jnp.zeros((8, D), F32)
    for i, v in enumerate((gain_grad_one, gain_grad_two, block_square, pool_square)):
        v = jnp.sum(v, axis=0, keepdims=True)
        if i >= 2:
            v = jnp.sum(v, axis=1, keepdims=True)
        small = jnp.where(line == i, v, small)
    s.terms[0] = small
    sum_s = summed(links, s.terms, s.term_in, partners)
    step(sum_s)
    drain(sum_q, sum_s, sum_d, sum_u, sum_p, sum_o)
    loads.copy(s.terms.at[len(partners)], s.small_out)
    links.finish()
    loads.finish()


IN_NAMES = (
    "tokens", "lengths", "w_qkv", "w_out", "w_up", "w_down", "w_pool",
    "gain_one", "gain_two", "pooled_grad", "cos_in", "sin_in",
)
OUT_NAMES = ("pooled_out", "gtok_out", "gq_out", "go_out", "gu_out", "gd_out", "gp_out", "small_out")


def tables(length):
    half = HEAD // 2
    frequency = np.exp(-math.log(10000.0) * np.arange(half) / half)
    angle = frequency[:, None] * np.arange(length)[None, :]
    return np.cos(angle).astype(np.float32), np.sin(angle).astype(np.float32)


def shards(tokens, lengths, w_qkv, w_out, w_up, w_down, w_pool, gain_one, gain_two, pooled_grad):
    T, D = tokens.shape
    HC, U = w_out.shape[0], w_up.shape[1]
    dp = lax.axis_size("dp")
    bits = dp.bit_length() - 1
    assert lax.axis_size("tensor") == 4 and lengths.shape == (2, 4) and dp == 1 << bits and bits > 0
    cos, sin = tables(2 * T)
    scratch = scratch_list(T, D, HC, U, bits)
    names = IN_NAMES + OUT_NAMES + tuple(n for n, _, _ in scratch) + ("send_sems", "recv_sems", "load_sems")
    hbm, vmem, smem = pl.BlockSpec(memory_space=pl.ANY), pl.BlockSpec(memory_space=pltpu.VMEM), pl.BlockSpec(memory_space=pltpu.SMEM)
    copies = 96 + 8 * bits
    outs = pl.pallas_call(
        functools.partial(kernel, bits, names),
        out_shape=[
            jax.ShapeDtypeStruct((T // POOL, D), BF16),
            jax.ShapeDtypeStruct((T, D), BF16),
            jax.ShapeDtypeStruct((3, D, HC), BF16),
            jax.ShapeDtypeStruct((HC, D), BF16),
            jax.ShapeDtypeStruct((D, U), BF16),
            jax.ShapeDtypeStruct((U, D), BF16),
            jax.ShapeDtypeStruct((POOL * D, D), BF16),
            jax.ShapeDtypeStruct((8, D), F32),
        ],
        in_specs=[hbm, smem, hbm, hbm, hbm, hbm, hbm, vmem, vmem, hbm, hbm, hbm],
        out_specs=[hbm] * 8,
        scratch_shapes=[pltpu.VMEM(shape, kind) for _, shape, kind in scratch]
        + [pltpu.SemaphoreType.DMA((copies,)), pltpu.SemaphoreType.DMA((copies,)), pltpu.SemaphoreType.DMA((32,))],
        compiler_params=pltpu.CompilerParams(
            collective_id=0, has_side_effects=True, vmem_limit_bytes=64 * 2**20 - 2**16
        ),
    )(
        tokens, lengths, jnp.transpose(w_qkv, (1, 0, 2)), w_out, w_up, w_down, w_pool,
        gain_one.reshape(1, D), gain_two.reshape(1, D), pooled_grad, cos, sin,
    )
    pooled, gtok, gq, go, gu, gd, gp, small = outs
    group = dp * 4 * T * D
    return (
        pooled,
        jnp.sqrt(small[2, 0] / group),
        jnp.sqrt(small[3, 0] / (group // POOL)),
        gtok,
        jnp.transpose(gq, (1, 0, 2)).astype(F32),
        go.astype(F32),
        gu.astype(F32),
        gd.astype(F32),
        gp.astype(F32),
        small[0],
        small[1],
    )


def solution(mesh):
    rows = P(("dp", "tensor"), None)
    placed = (
        rows, P("dp", None), P(None, None, "tensor"), P("tensor", None), P(None, "tensor"),
        P("tensor", None), P(), P(), P(), rows,
    )
    return jax.shard_map(
        shards,
        mesh=mesh,
        in_specs=placed,
        out_specs=(
            rows, P(), P(), rows, P(None, None, "tensor"), P("tensor", None), P(None, "tensor"),
            P("tensor", None), P(), P(), P(),
        ),
        check_vma=False,
    )
```

time: 596 us -> 167 us (0.28)
  waiting for transfers between devices: 227 us -> 0 us
  matrix products: 155 us -> 0 us
  Pallas kernels: 0 us -> 150 us
  other arithmetic: 69.5 us -> 7.43 us
  blocking collectives: 54.7 us -> 0 us
  local copies, waits for them, and re-layouts: 38 us -> 4.25 us
  starting transfers between devices: 27.8 us -> 0 us
  between operations: 18.2 us -> 4.32 us
    psum x1 -> x0, waiting for transfers between devices: 217 us -> none  [shards(): lax.psum((grad_qkv_full, grad_out_full, grad_up_full, grad_down_full, gra...]
    dot_general x21 -> x0, matrix products: 155 us -> none  [the longest x1 28.8 us: one_block(): jnp.einsum('qhe,khe->hqk', grad_mixed, values, preferred_element_type=jnp...]
    pallas_call x0 -> x1, Pallas kernels: none -> 150 us  [shards(): pl.pallas_call(functools.partial(kernel, bits, names), out_shape=[jax.Sha...]
    psum x1 -> x0, blocking collectives: 44.9 us -> none  [shards(): lax.psum((grad_qkv_full, grad_out_full, grad_up_full, grad_down_full, gra...]
    ppermute x6 -> x0, starting transfers between devices: 27.6 us -> none  [passed_along(): return lax.ppermute(block, axis, route)]
    convert_element_type x3 -> x5, other arithmetic: 34.5 us -> 7.43 us  [the longest x1 3.57 us: shards(): gp.astype(F32)]
    reduce_sum x3 -> x0, other arithmetic: 17.5 us -> none  [the longest x1 17.2 us: one_block(): row_total = jnp.sum(exp_scores, axis=2, keepdims=True)]
    all_gather x1 -> x0, blocking collectives: 9.83 us -> none  [shards(): lax.all_gather(w_out, 'tensor', axis=0, tiled=True)]
  transfers between devices with their start and end apart: 10 -> 0, of which waited for: 2 -> 0; matrix products, arithmetic and copies ran while one was open for 39% -> 0% of each run, Pallas kernels for 0% -> 0%
where the time goes in v1:
time: 167 us; the launch traced here: 166 us
  Pallas kernels  150 us (90%)
  other arithmetic  7.43 us (4%)
  between operations  4.32 us (3%)
  local copies, waits for them, and re-layouts  4.25 us (3%)
    pallas_call x1, Pallas kernels, shards(): pl.pallas_call(functools.partial(kernel, bits, names), out_shape=[jax.Sha...  150 us
    convert_element_type x1, other arithmetic, shards(): gp.astype(F32)  3.57 us

profile of v1, /device:TPU:0, one launch (start us, length us, event | category | flops | bytes accessed | tf_op | source)
XLA Modules:
  0.0 166.2 jit_solution(794679562777092686)
XLA Ops:
  0.6 150.2 %shard_map.203 = (bf16[256,512]{1,0:T(8,128)(2,1)}, bf16[768,512]{1,0:T(8,128)(2,1)}, bf16[3,512,128]{2,1,0:T(8,128)(2,1)}, bf16[128,512]{1,0:T(8,128)(2,1)}, bf...) custom-call(bf16[768,512]{1,0:T(8,128)(2,1)} %refs_0_.1, ...), custom_call_target="tpu_custom_call" | custom-call | tf_op jit(solution)/shard_map/pallas_call | solution.py:650
  150.9 1.4 fusion
  152.3 1.3 fusion.1
  154.9 0.0 copy-start.2
  154.9 3.6 %convert_element_type.23 = f32[1536,512]{1,0:T(8,128)} convert(bf16[1536,512]{1,0:T(8,128)(2,1)} %get-tuple-element.26) | non-fusion elementwise | flops 786432 | bytes 4718592 | tf_op jit(solution)/shard_map/convert_element_type | solution.py:684
  158.5 0.0 copy-start.1
  158.5 0.0 copy-done.2
  158.5 0.0 copy-start.3
  158.5 1.1 convert_element_type.21
  159.6 0.0 copy-start.5
  159.6 0.0 copy-done.1
  159.6 0.0 copy-start.4
  159.6 0.0 copy-start
  159.6 1.1 convert_element_type.22
  160.7 0.0 copy-done.3
  160.7 0.9 convert_bitcast_fusion
  161.7 0.0 copy-done.5
  161.7 0.7 convert_element_type.20
  162.4 0.0 copy-done.4
  162.4 0.7 copy.25
  163.1 0.0 copy-done
  163.1 0.9 copy.26
Async XLA Ops:
  154.9 3.6 %copy-start.2 = (bf16[512,512]{1,0:T(8,128)(2,1)S(1)}, bf16[512,512]{1,0:T(8,128)(2,1)}, u32[]{:S(2)}) copy-start(bf16[512,512]{1,0:T(8,128)(2,1)} %get-tuple-element.24) | copy-start | bytes 1572868
  158.5 1.1 copy-start.1
  158.5 2.2 %copy-start.3 = (bf16[3,512,128]{2,1,0:T(8,128)(2,1)S(1)}, bf16[3,512,128]{2,1,0:T(8,128)(2,1)}, u32[]{:S(2)}) copy-start(bf16[3,512,128]{2,1,0:T(8,128)(2,1)} %get-tuple-element.22) | copy-start | bytes 1179652
  159.6 2.0 %copy-start.5 = (bf16[128,512]{1,0:T(8,128)(2,1)S(1)}, bf16[128,512]{1,0:T(8,128)(2,1)}, u32[]{:S(2)}) copy-start(bf16[128,512]{1,0:T(8,128)(2,1)} %get-tuple-element.23) | copy-start | bytes 393220
  159.6 2.8 %copy-start.4 = (bf16[256,512]{1,0:T(8,128)(2,1)S(1)}, bf16[256,512]{1,0:T(8,128)(2,1)}, u32[]{:S(2)}) copy-start(bf16[256,512]{1,0:T(8,128)(2,1)} %get-tuple-element.42) | copy-start | bytes 786436
  159.6 3.5 %copy-start = (bf16[768,512]{1,0:T(8,128)(2,1)S(1)}, bf16[768,512]{1,0:T(8,128)(2,1)}, u32[]{:S(2)}) copy-start(bf16[768,512]{1,0:T(8,128)(2,1)} %get-tuple-element.45) | copy-start | bytes 2359300
